TPU v7x, 128 devices: a whole 4x4x4 slice. The times are simulated.
128 devices in a mesh: dp: 8 (over z, core), mp: 16 (over y, x).
Axes of the slice: x: 4, y: 4, z: 4, core: 2. Of those that a mesh axis runs over, the one named last changes fastest.
Arguments:
- gradient: bfloat16 [80, 262144], P(None, ('dp', 'mp')), may hold values from -1500 to 1500
- owner_device: int32 [80], replicated, may hold values from 0 to 127, as said below
- state_slot: int32 [80], replicated, may hold values from 0 to 1
- left_stat: float32 [256, 512, 512], P(('dp', 'mp')), may hold values from -8 to 10, as said below
- right_stat: float32 [256, 512, 512], P(('dp', 'mp')), may hold values from -8 to 10, as said below
- left_basis: float32 [256, 512, 512], P(('dp', 'mp')), may hold values from -1 to 1, as said below
- right_basis: float32 [256, 512, 512], P(('dp', 'mp')), may hold values from -1 to 1, as said below
- moment: float32 [256, 512, 512], P(('dp', 'mp')), may hold values from -4 to 4
- second_moment: float32 [256, 512, 512], P(('dp', 'mp')), may hold values from 0.2 to 5
Outputs:
- new_left_stat: float32 [256, 512, 512], P(('dp', 'mp'))
- new_right_stat: float32 [256, 512, 512], P(('dp', 'mp'))
- new_left_basis: float32 [256, 512, 512], P(('dp', 'mp'))
- new_right_basis: float32 [256, 512, 512], P(('dp', 'mp'))
- new_moment: float32 [256, 512, 512], P(('dp', 'mp'))
- new_second_moment: float32 [256, 512, 512], P(('dp', 'mp'))
- direction: float32 [80, 262144], P(None, ('dp', 'mp'))
Inputs may be any that keep to these rules, and one draw needn't show every extreme that they name: Block b's state is slot state_slot[b] of device owner_device[b], devices counted in dp+mp order; no two blocks share a slot. Devices 2k and 2k + 1 hold at most 2 blocks together, the first two and the last two devices hold one block each, and some devices hold 2. `left_stat`: symmetric positive definite. `right_stat`: symmetric positive definite. `left_basis`: orthogonal matrices. `right_basis`: orthogonal matrices.
All inputs are finite; a program needn't handle non-finite values.
Results may differ from a plain program's by a relative error of at most 0.0003.
Values may be sent and summed in bfloat16 or wider, within the bound.
A program may use at most 128 MiB of HBM per device.

v0:
```python
import functools

import jax
import jax.numpy as jnp
from jax import lax
from jax.experimental import pallas as pl
from jax.experimental.pallas import tpu as pltpu
from jax.sharding import PartitionSpec as P

N = 512
D = 128
LB = 32
PIECE = 2048
F32 = jnp.float32
BF16 = jnp.bfloat16
KEEP = 0.9
MIX = 1.0 - KEEP
STABILITY = 1e-08


def split(x):
    hi = x.astype(BF16)
    lo = (x - hi.astype(F32)).astype(BF16)
    return hi, lo


def dot3(a, b, ca, cb):
    dims = (((ca,), (cb,)), ((), ()))
    d = lambda x, y: lax.dot_general(x, y, dims, preferred_element_type=F32)
    return d(a[0], b[0]) + (d(a[0], b[1]) + d(a[1], b[0]))


def finish(ws, s, lb):
    lanes = lax.broadcasted_iota(jnp.int32, (lb, D), 1)
    on = lanes == lax.broadcasted_iota(jnp.int32, (lb, D), 0) + s * lb
    out = []
    for d, e in ws:
        piv = jnp.sum(jnp.where(on, d, 0.0), axis=1, keepdims=True)
        r = lax.rsqrt(piv)
        out.append((d * r, e * r))
    return out


def leaf(ws, s, lb):
    n = len(ws)
    sub = lax.broadcasted_iota(jnp.int32, (8, D), 0)
    ng = lb // 8
    ws = [([d[8 * i:8 * i + 8] for i in range(ng)], [e[8 * i:8 * i + 8] for i in range(ng)]) for d, e in ws]
    for g in range(ng):
        bc = []
        for b in range(n):
            ds, es = ws[b]
            bc.append([[jnp.broadcast_to(ds[i][:, s * lb + 8 * g + j:s * lb + 8 * g + j + 1], (8, D)) for i in range(g, ng)] for j in range(8)])
        for k in range(8):
            for b in range(n):
                ds, es = ws[b]
                cols = bc[b]
                own = cols[k]
                rp = 1.0 / jnp.broadcast_to(own[0][k:k + 1, :], (8, D))
                m = [x * rp for x in own]
                m[0] = jnp.where(sub > k, m[0], 0.0)
                for j in range(k + 1, 8):
                    w = jnp.broadcast_to(own[0][j:j + 1, :], (8, D))
                    cols[j] = [x - y * w for x, y in zip(cols[j], m)]
                rd = jnp.broadcast_to(ds[g][k:k + 1, :], (8, D))
                re = jnp.broadcast_to(es[g][k:k + 1, :], (8, D))
                for i in range(g, ng):
                    if i == g and k == 7:
                        continue
                    ds[i] = ds[i] - m[i - g] * rd
                    es[i] = es[i] - m[i - g] * re
    ws = [(jnp.concatenate(ds, axis=0), jnp.concatenate(es, axis=0)) for ds, es in ws]
    return finish(ws, s, lb)


def factor_body(nm, lb, a_ref, p_ref, q_ref, w_d, w_e):
    eye = (lax.broadcasted_iota(jnp.int32, (D, D), 0) == lax.broadcasted_iota(jnp.int32, (D, D), 1)).astype(F32)

    def step(k, carry):
        at = pl.ds(pl.multiple_of(k * D, D), D)
        for b in range(nm):
            w_d[b] = a_ref[b, at, at]
            w_e[b] = eye
        for s in range(D // lb):
            here = slice(s * lb, (s + 1) * lb)
            ws = [(w_d[b, here, :], w_e[b, here, :]) for b in range(nm)]
            ws = leaf(ws, s, lb)
            for b in range(nm):
                rd, re = ws[b]
                w_e[b, here, :] = re
                if s < D // lb - 1:
                    low = slice((s + 1) * lb, D)
                    dh, dl = split(rd)
                    eh, el = split(re)
                    lhs = jnp.concatenate([dh, dh, dl], axis=0)
                    rhs_d = jnp.concatenate([dh, dl, dh], axis=0)
                    rhs_e = jnp.concatenate([eh, el, eh], axis=0)
                    dims = (((0,), (0,)), ((), ()))
                    ud = lax.dot_general(lhs, rhs_d, dims, preferred_element_type=F32)
                    ue = lax.dot_general(lhs, rhs_e, dims, preferred_element_type=F32)
                    w_d[b, low, :] = w_d[b, low, :] - ud[(s + 1) * lb:, :]
                    w_e[b, low, :] = w_e[b, low, :] - ue[(s + 1) * lb:, :]
        for kk in range(N // D):
            @pl.when(k == kk)
            def _():
                o = kk * D
                for b in range(nm):
                    x = split(w_e[b])
                    q = dot3(split(p_ref[b, :, o:o + D]), x, 1, 1)
                    q_ref[b, :, o:o + D] = q
                    if kk < N // D - 1:
                        r = split(dot3(x, split(a_ref[b, o:o + D, o + D:]), 1, 0))
                        a_ref[b, o + D:, o + D:] = a_ref[b, o + D:, o + D:] - dot3(r, r, 0, 0)
                        p_ref[b, :, o + D:] = p_ref[b, :, o + D:] - dot3(split(q), r, 1, 0)
        return carry

    lax.fori_loop(0, N // D, step, 0)


def dot2(a, b, ca, cb):
    dims = (((ca,), (cb,)), ((), ()))
    d = lambda x, y: lax.dot_general(x, y, dims, preferred_element_type=F32)
    return d(a, b[0]) + d(a, b[1])


def dot2l(a, b, ca, cb):
    dims = (((ca,), (cb,)), ((), ()))
    d = lambda x, y: lax.dot_general(x, y, dims, preferred_element_type=F32)
    return d(a[0], b) + d(a[1], b)


def ahead_kernel(ls, rs, lb, rb, m, pl_out, pr_out, m2_out):
    l, r = split(lb[0]), split(rb[0])
    pl_out[0] = KEEP * dot3(split(ls[0]), l, 1, 0)
    pr_out[0] = KEEP * dot3(split(rs[0]), r, 1, 0)
    m2_out[0] = dot3(split(dot3(l, split(m[0]), 0, 0)), r, 1, 0)


def ahead(left_stat, right_stat, left_basis, right_basis, moment):
    one = pl.BlockSpec((1, N, N), lambda s: (s, 0, 0))
    return pl.pallas_call(
        ahead_kernel,
        grid=(2,),
        out_shape=[jax.ShapeDtypeStruct((2, N, N), F32)] * 3,
        in_specs=[one] * 5,
        out_specs=[one] * 3,
        compiler_params=pltpu.CompilerParams(vmem_limit_bytes=56 << 20),
        cost_estimate=pl.CostEstimate(flops=24 * 2 * N**3, bytes_accessed=16 * N * N * 4, transcendentals=0),
        name="ahead",
    )(left_stat, right_stat, left_basis, right_basis, moment)


def rotate_kernel(live, arr, lb, rb, m2, second, g_out, t_out, u_out, second_out, step_out, clip_out, x_s):
    s = pl.program_id(0)
    alive = live[s] > 0
    lanes = lax.broadcasted_iota(jnp.int32, (D, D), 1)
    terms = jnp.where(lanes < 3, arr[0, :, PIECE:].astype(F32), 0.0)
    total = jnp.sum(jnp.sum(terms, axis=1, keepdims=True), axis=0, keepdims=True)
    mean = total / (80.0 * N * N)
    clip = 1.0 / jnp.maximum(1.0, jnp.sqrt(mean))
    clip_out[...] = jnp.broadcast_to(clip, (8, D))
    for q in range(4):
        for c in range(4):
            x_s[c, pl.ds(q, D, stride=4), :] = arr[0, :, q * N + c * D:q * N + (c + 1) * D].astype(F32)
    g = jnp.concatenate([x_s[c] for c in range(4)], axis=1).astype(BF16)
    g_out[0] = g
    l, r = split(lb[0]), split(rb[0])
    t = dot2l(l, g, 0, 0)
    t_out[0] = t
    u_out[0] = dot2(g, r, 1, 0)
    rot = clip * dot3(split(t), r, 1, 0)
    v = KEEP * second[0] + MIX * rot * rot
    second_out[0] = jnp.where(alive, v, second[0])
    ratio = (KEEP * m2[0] + MIX * rot) / (jnp.sqrt(v) + STABILITY)
    step = dot3(split(dot3(l, split(ratio), 1, 0)), r, 1, 1)
    step = jnp.where(alive, step, 0.0)
    for c in range(4):
        x_s[c] = step[:, c * D:(c + 1) * D]
        for q in range(4):
            step_out[0, :, q * N + c * D:q * N + (c + 1) * D] = x_s[c, pl.ds(q, D, stride=4), :]


def rotate(live, arrived, left_basis, right_basis, m2, second):
    one = pl.BlockSpec((1, N, N), lambda s: (s, 0, 0))
    width = arrived.shape[-1]
    return pl.pallas_call(
        rotate_kernel,
        grid=(2,),
        out_shape=[
            jax.ShapeDtypeStruct((2, N, N), BF16),
            jax.ShapeDtypeStruct((2, N, N), F32),
            jax.ShapeDtypeStruct((2, N, N), F32),
            jax.ShapeDtypeStruct((2, N, N), F32),
            jax.ShapeDtypeStruct((2, D, PIECE), F32),
            jax.ShapeDtypeStruct((8, D), F32),
        ],
        in_specs=[
            pl.BlockSpec(memory_space=pltpu.SMEM),
            pl.BlockSpec((1, D, width), lambda s: (s, 0, 0)),
            one, one, one, one,
        ],
        out_specs=[one] * 4 + [
            pl.BlockSpec((1, D, PIECE), lambda s: (s, 0, 0)),
            pl.BlockSpec((8, D), lambda s: (0, 0)),
        ],
        scratch_shapes=[pltpu.VMEM((4, N, D), F32)],
        compiler_params=pltpu.CompilerParams(vmem_limit_bytes=56 << 20),
        cost_estimate=pl.CostEstimate(flops=30 * 2 * N**3, bytes_accessed=20 * N * N * 4, transcendentals=0),
        name="rotate",
    )(live, arrived, left_basis, right_basis, m2, second)


def refresh_kernel(live, clip_ref, g_ref, t_ref, u_ref, pl_ref, pr_ref, ls_h, rs_h, lb_h, rb_h, m_h,
                   nls_h, nrs_h, nlb_h, nrb_h, nm_h,
                   a_ref, p_ref, q_ref, w_d, w_e, st, bs, mo, in_sem, out_sem):
    ins = [(ls_h, st.at[pl.ds(0, 2)]), (rs_h, st.at[pl.ds(2, 2)]), (m_h, mo), (lb_h, bs.at[pl.ds(0, 2)]), (rb_h, bs.at[pl.ds(2, 2)])]
    loads = [pltpu.make_async_copy(src, dst, in_sem.at[i]) for i, (src, dst) in enumerate(ins)]
    for c in loads:
        c.start()
    clip = clip_ref[0:1, 0:1]
    weight = (MIX / N) * clip * clip
    for s in range(2):
        g = g_ref[s]
        p = pl_ref[s] + weight * dot2(g, split(t_ref[s]), 1, 1)
        p_ref[s] = p
        p = split(p)
        a_ref[s] = dot3(p, p, 0, 0)
        p = pr_ref[s] + weight * dot2(g, split(u_ref[s]), 0, 0)
        p_ref[2 + s] = p
        p = split(p)
        a_ref[2 + s] = dot3(p, p, 0, 0)
    for c in loads[:3]:
        c.wait()
    for s in range(2):
        alive = live[s] > 0
        g = g_ref[s]
        one = lambda c: lax.dot_general(g, g, (((c,), (c,)), ((), ())), preferred_element_type=F32)
        st[s] = jnp.where(alive, KEEP * st[s] + weight * one(1), st[s])
        st[2 + s] = jnp.where(alive, KEEP * st[2 + s] + weight * one(0), st[2 + s])
        mo[s] = jnp.where(alive, KEEP * mo[s] + (MIX * clip) * g.astype(F32), mo[s])
    outs = [(st.at[pl.ds(0, 2)], nls_h), (st.at[pl.ds(2, 2)], nrs_h), (mo, nm_h)]
    stores = [pltpu.make_async_copy(src, dst, out_sem.at[i]) for i, (src, dst) in enumerate(outs)]
    for c in stores:
        c.start()
    factor_body(4, LB, a_ref, p_ref, q_ref, w_d, w_e)
    for c in loads[3:]:
        c.wait()
    for s in range(2):
        alive = live[s] > 0
        q_ref[s] = jnp.where(alive, q_ref[s], bs[s])
        q_ref[2 + s] = jnp.where(alive, q_ref[2 + s], bs[2 + s])
    outs = [(q_ref.at[pl.ds(0, 2)], nlb_h), (q_ref.at[pl.ds(2, 2)], nrb_h)]
    last = [pltpu.make_async_copy(src, dst, out_sem.at[3 + i]) for i, (src, dst) in enumerate(outs)]
    for c in last:
        c.start()
    for c in stores + last:
        c.wait()


def refresh(live, clip, g, t, u, p_left, p_right, left_stat, right_stat, left_basis, right_basis, moment):
    vm = pl.BlockSpec(memory_space=pltpu.VMEM)
    hb = pl.BlockSpec(memory_space=pl.ANY)
    return pl.pallas_call(
        refresh_kernel,
        out_shape=[jax.ShapeDtypeStruct((2, N, N), F32)] * 5,
        in_specs=[pl.BlockSpec(memory_space=pltpu.SMEM)] + [vm] * 6 + [hb] * 5,
        out_specs=[hb] * 5,
        scratch_shapes=[
            pltpu.VMEM((4, N, N), F32),
            pltpu.VMEM((4, N, N), F32),
            pltpu.VMEM((4, N, N), F32),
            pltpu.VMEM((4, D, D), F32),
            pltpu.VMEM((4, D, D), F32),
            pltpu.VMEM((4, N, N), F32),
            pltpu.VMEM((4, N, N), F32),
            pltpu.VMEM((2, N, N), F32),
            pltpu.SemaphoreType.DMA((5,)),
            pltpu.SemaphoreType.DMA((5,)),
        ],
        compiler_params=pltpu.CompilerParams(vmem_limit_bytes=56 << 20),
        cost_estimate=pl.CostEstimate(flops=100 * 2 * N**3, bytes_accessed=30 * N * N * 4, transcendentals=0),
        name="refresh",
    )(live, clip, g, t, u, p_left, p_right, left_stat, right_stat, left_basis, right_basis, moment)


def shards(
    gradient,
    owner_device,
    state_slot,
    left_stat,
    right_stat,
    left_basis,
    right_basis,
    moment,
    second_moment,
):
    devices = lax.axis_size(("dp", "mp"))
    slot_count = left_stat.shape[0]
    flat_piece = gradient.shape[1]
    my_index = lax.axis_index(("dp", "mp"))
    own_square = jnp.sum(jnp.square(gradient.astype(F32)))
    first = own_square.astype(BF16)
    second = (own_square - first.astype(F32)).astype(BF16)
    third = (own_square - first.astype(F32) - second.astype(F32)).astype(BF16)
    terms = jnp.stack([first, second, third])
    slot_code = state_slot * devices + owner_device
    picker = (
        slot_code[None, :] == jnp.arange(slot_count * devices, dtype=jnp.int32)[:, None]
    ).astype(BF16)
    outgoing = jnp.dot(picker, gradient, preferred_element_type=F32).astype(BF16)
    outgoing = outgoing.reshape(slot_count, devices, flat_piece)
    tail = jnp.broadcast_to(jnp.pad(terms, (0, 125)), (slot_count, devices, 128))
    outgoing = jnp.concatenate([outgoing, tail], axis=2)
    arrived = lax.all_to_all(outgoing, ("dp", "mp"), split_axis=1, concat_axis=1, tiled=True)
    p_left, p_right, rotated_old = ahead(left_stat, right_stat, left_basis, right_basis, moment)
    live = jnp.any(
        (owner_device[None, :] == my_index)
        & (state_slot[None, :] == jnp.arange(slot_count, dtype=jnp.int32)[:, None]),
        axis=1,
    ).astype(jnp.int32)
    g, t, u, new_second, steps, clip = rotate(
        live, arrived, left_basis, right_basis, rotated_old, second_moment
    )
    backward = lax.all_to_all(steps, ("dp", "mp"), split_axis=1, concat_axis=1, tiled=True)
    new_left, new_right, new_left_basis, new_right_basis, new_moment = refresh(
        live, clip, g, t, u, p_left, p_right, left_stat, right_stat, left_basis, right_basis, moment
    )
    direction = jnp.take(backward.reshape(slot_count * devices, flat_piece), slot_code, axis=0)
    return (
        new_left,
        new_right,
        new_left_basis,
        new_right_basis,
        new_moment,
        new_second,
        direction,
    )


def solution(mesh):
    spread = P(("dp", "mp"), None, None)
    flat = P(None, ("dp", "mp"))
    return jax.shard_map(
        shards,
        mesh=mesh,
        in_specs=(flat, P(), P()) + (spread,) * 6,
        out_specs=(spread,) * 6 + (flat,),
        check_vma=False,
    )
```

profile of v0, /device:TPU:1, one launch (start us, length us, event | category | flops | bytes accessed | tf_op | source)
XLA Modules:
  0.0 114.7 jit_solution(12793893858329844003)
XLA Ops:
  0.6 1.7 %multiply_reduce_fusion = f32[]{:T(128)} fusion(bf16[80,2048]{1,0:T(8,128)(2,1)} %param.9), kind=kLoop, calls=%fused_computation.3 | loop fusion | flops 491519 | bytes 327684 | tf_op jit(solution)/shard_map/reduce_sum | solution.py:301
  3.7 0.7 compare_and_fusion
  4.4 1.4 %convolution_convert_fusion = bf16[256,2048]{1,0:T(8,128)(2,1)S(1)} fusion(bf16[80,2048]{1,0:T(8,128)(2,1)} %param.9, s32[80]{0:T(128)S(1)} %get-tuple-element.36), kind=kOutput, calls=%fused_computation.1 | convolution fusion | flops 84430848 | bytes 1376576 | tf_op jit(solution)/shard_map/dot_general | solution.py:310
  5.8 1.1 copy.20
  6.9 0.1 select_maximum_fusion
  7.0 0.0 copy-start
  7.0 2.1 %pad_maximum_fusion = bf16[2,128,2176]{2,0,1:T(2,128)(2,1)} fusion(bf16[2,128,2048]{2,0,1:T(2,128)(2,1)S(1)} %copy.20, bf16[2176]{0:T(1024)(128)(2,1)S(1)} %pad.6.clone), kind=kLoop, calls=%fused_computation.2 | loop fusion | flops 2228224 | bytes 2167040 | tf_op jit(solution)/shard_map/concatenate | solution.py:313
  9.1 11.5 %all-to-all-start = ((bf16[2,128,2176]{2,0,1:T(2,128)(2,1)}), bf16[2,128,2176]{2,0,1:T(2,128)(2,1)S(1)}, u32[]{:S(2)}, u32[]{:S(2)}) async-start(bf16[2,128,2176]{2,0,1:T(2,128)(2,1)} %pad_maximum_fusion), calls=%async_computation | async-start | bytes 2228224 | tf_op jit(solution)/shard_map/all_to_all | solution.py:314
  20.6 0.0 copy-done
  20.6 0.1 and_reduce_fusion
  20.7 0.5 convert_element_type.28.live
  21.2 10.4 %ahead.1 = (f32[2,512,512]{2,1,0:T(8,128)}, f32[2,512,512]{2,1,0:T(8,128)}, f32[2,512,512]{2,1,0:T(8,128)}) custom-call(f32[2,512,512]{2,1,0:T(8,128)} %ls_h.1, f32[2,512,512]{2,1,0:T(8,128)} %rs_h.1, f32[2,512,512]{2,1,0:T(8,128)} %lb_h.1, f32[2,512,512]{2,1,0:T(8,128)} %rb_h.1, f32[2,512,512]{2,1,0:T(8,128)} %m_h.1), custom_call_target="tpu_custom_call" | custom-call | flops 6442450944 | bytes 16777216 | tf_op jit(solution)/shard_map/ahead/pallas_call | solution.py:141
  31.6 8.4 %all-to-all-done = bf16[2,128,2176]{2,0,1:T(2,128)(2,1)S(1)} async-done(((bf16[2,128,2176]{2,0,1:T(2,128)(2,1)}), bf16[2,128,2176]{2,0,1:T(2,128)(2,1)S(1)}, u32[]{:S(2)}, u32[]{:S(2)}) %all-to-all-start) | async-done | bytes 1114144 | tf_op jit(solution)/shard_map/all_to_all | solution.py:314
  40.0 1.1 copy.21.arr
  41.1 12.4 %rotate.1 = (bf16[2,512,512]{2,1,0:T(8,128)(2,1)}, f32[2,512,512]{2,1,0:T(8,128)}, f32[2,512,512]{2,1,0:T(8,128)}, f32[2,512,512]{2,1,0:T(8,128)}, f32[2,128,2048]{2,1,0:T(8,128)}, /*index=5*/f32[8,128]{1,0:T(8,128)}) custom-call(s32[2]{0:T(128)} %convert_element_type.28.live, bf16[2,128,2176]{2,1,0:T(8,128)(2,1)} %copy.21.arr, f32[2,512,512]{2,1,0:T(8,128)} %lb_h.1, ...), custom_call_target="tpu_custom_call" | custom-call | flops 8053063680 | bytes 20971520 | tf_op jit(solution)/shard_map/rotate/pallas_call | solution.py:186
  53.5 4.5 %copy.22 = f32[2,128,2048]{2,0,1:T(2,128)} copy(f32[2,128,2048]{2,1,0:T(8,128)} %get-tuple-element.34) | data formatting | bytes 4194304 | tf_op jit(solution)/shard_map/rotate/pallas_call | solution.py:186
  58.0 6.0 %all-to-all-start.1 = ((f32[2,128,2048]{2,0,1:T(2,128)}), f32[2,128,2048]{2,0,1:T(2,128)}, u32[]{:S(2)}, u32[]{:S(2)}) async-start(f32[2,128,2048]{2,0,1:T(2,128)} %copy.22), calls=%async_computation.1 | async-start | bytes 4194304 | tf_op jit(solution)/shard_map/all_to_all | solution.py:324
  64.0 46.1 %refresh.1 = (f32[2,512,512]{2,1,0:T(8,128)}, f32[2,512,512]{2,1,0:T(8,128)}, f32[2,512,512]{2,1,0:T(8,128)}, f32[2,512,512]{2,1,0:T(8,128)}, f32[2,512,512]{2,1,0:T(8,128)}) custom-call(s32[2]{0:T(128)} %convert_element_type.28.live, f32[8,128]{1,0:T(8,128)} %get-tuple-element.22.clip_ref, bf16[2,512,512]{2,1,0:T(8,128)(2,1)} %get-tuple-element.23.g_ref, ...), custom_call_target="tpu_custom_call" | custom-call | flops 26843545600 | bytes 31457280 | tf_op jit(solution)/shard_map/refresh/pallas_call | solution.py:263
  110.1 0.0 all-to-all-done.1
  110.2 2.8 %copy.23 = f32[2,128,2048]{2,1,0:T(8,128)S(1)} copy(f32[2,128,2048]{2,0,1:T(2,128)} %all-to-all-done.1) | data formatting | bytes 4194304 | tf_op jit(solution)/shard_map/all_to_all | solution.py:324
  113.0 0.8 gather_fusion
  113.8 0.9 broadcast_select_fusion
  (3 shorter events, 0.0 us)
Async XLA Ops:
  7.0 13.6 %copy-start = (s32[80]{0:T(128)S(1)}, s32[80]{0:T(128)}, u32[]{:S(2)}) copy-start(s32[80]{0:T(128)} %param.11) | copy-start | bytes 964
  9.1 30.9 %all-to-all-start = ((bf16[2,128,2176]{2,0,1:T(2,128)(2,1)}), bf16[2,128,2176]{2,0,1:T(2,128)(2,1)S(1)}, u32[]{:S(2)}, u32[]{:S(2)}) async-start(bf16[2,128,2176]{2,0,1:T(2,128)(2,1)} %pad_maximum_fusion), calls=%async_computation | async-start | bytes 2228224 | tf_op jit(solution)/shard_map/all_to_all | solution.py:314
  58.0 52.1 %all-to-all-start.1 = ((f32[2,128,2048]{2,0,1:T(2,128)}), f32[2,128,2048]{2,0,1:T(2,128)}, u32[]{:S(2)}, u32[]{:S(2)}) async-start(f32[2,128,2048]{2,0,1:T(2,128)} %copy.22), calls=%async_computation.1 | async-start | bytes 4194304 | tf_op jit(solution)/shard_map/all_to_all | solution.py:324
where the time goes:
time: 115 us
  Pallas kernels  68.8 us (60%)
  starting transfers between devices  17.5 us (15%)
  local copies, waits for them, and re-layouts  10.3 us (9%)
  waiting for transfers between devices  8.44 us (7%)
  other arithmetic  6.19 us (5%)
  between operations  2.03 us (2%)
  matrix products  1.39 us (1%)
    pallas_call x1, Pallas kernels, refresh(): pl.pallas_call(refresh_kernel, out_shape=[jax.ShapeDtypeStruct((2, N, N),...  46.1 us
    pallas_call x1, Pallas kernels, rotate(): pl.pallas_call(rotate_kernel, grid=(2,), out_shape=[jax.ShapeDtypeStruct(...  12.4 us
    all_to_all x1, starting transfers between devices, shards(): lax.all_to_all(outgoing, ('dp', 'mp'), split_axis=1, concat_axis=1, tiled...  11.5 us
    pallas_call x1, Pallas kernels, ahead(): pl.pallas_call(ahead_kernel, grid=(2,), out_shape=[jax.ShapeDtypeStruct((...  10.4 us
    all_to_all x1, waiting for transfers between devices, shards(): lax.all_to_all(outgoing, ('dp', 'mp'), split_axis=1, concat_axis=1, tiled...  8.44 us
    all_to_all x1, starting transfers between devices, shards(): lax.all_to_all(steps, ('dp', 'mp'), split_axis=1, concat_axis=1, tiled=True)  6.04 us
    pallas_call x1, local copies, waits for them, and re-layouts, rotate(): pl.pallas_call(rotate_kernel, grid=(2,), out_shape=[jax.ShapeDtypeStruct(...  4.52 us
    all_to_all x1, local copies, waits for them, and re-layouts, shards(): lax.all_to_all(steps, ('dp', 'mp'), split_axis=1, concat_axis=1, tiled=True)  2.81 us
  transfers between devices with their start and end apart: 2, of which 1 were waited for; matrix products, arithmetic and copies ran while one was open for 1% of the time, Pallas kernels for 49%

commit v1 on v0

--- a/solution.py
+++ b/solution.py
@@ -129,41 +129,126 @@
     return d(a[0], b) + d(a[1], b)
 
 
-def ahead_kernel(ls, rs, lb, rb, m, pl_out, pr_out, m2_out):
-    l, r = split(lb[0]), split(rb[0])
-    pl_out[0] = KEEP * dot3(split(ls[0]), l, 1, 0)
-    pr_out[0] = KEEP * dot3(split(rs[0]), r, 1, 0)
-    m2_out[0] = dot3(split(dot3(l, split(m[0]), 0, 0)), r, 1, 0)
-
-
-def ahead(left_stat, right_stat, left_basis, right_basis, moment):
-    one = pl.BlockSpec((1, N, N), lambda s: (s, 0, 0))
+def ahead_kernel(devices, mp, code, grad, ls_h, rs_h, lb_h, rb_h, m_h, pl_h, pr_h, m2_h, g_out, clip_out,
+                 stage, away, arr, x_s, st, bs, mo, res, in_sem, out_sem, send_sem, recv_sem):
+    me = lax.axis_index("dp") * mp + lax.axis_index("mp")
+    place = lambda d: {"dp": lax.div(d, mp), "mp": lax.rem(d, mp)}
+    barrier = pltpu.get_barrier_semaphore()
+
+    def greet(i, carry):
+        pl.semaphore_signal(barrier, inc=1, device_id=place(lax.rem(me + i, devices)), device_id_type=pl.DeviceIdType.MESH)
+        return carry
+
+    lax.fori_loop(1, devices, greet, 0)
+    ins = [(lb_h, bs.at[pl.ds(0, 2)]), (ls_h, st.at[pl.ds(0, 2)]), (rb_h, bs.at[pl.ds(2, 2)]), (rs_h, st.at[pl.ds(2, 2)]), (m_h, mo)]
+    loads = [pltpu.make_async_copy(src, dst, in_sem.at[n]) for n, (src, dst) in enumerate(ins)]
+    for c in loads:
+        c.start()
+
+    g = grad[...]
+    gf = g.astype(F32)
+    own = jnp.sum(jnp.sum(gf * gf, axis=1, keepdims=True), axis=0, keepdims=True)
+    first = own.astype(BF16).astype(F32)
+    second = (own - first).astype(BF16).astype(F32)
+    third = own - first - second
+    rows = lax.broadcasted_iota(jnp.int32, (16, D), 0)
+    tile = jnp.where(rows == 0, first, jnp.where(rows == 1, second, jnp.where(rows == 2, third, 0.0))).astype(BF16)
+    for s in range(2):
+        names = lax.broadcasted_iota(jnp.int32, (devices, code.shape[1]), 0) + s * devices
+        picker = (names == code[...]).astype(BF16)
+        row = jnp.dot(picker, g, preferred_element_type=F32)
+        for r in range(16):
+            stage[s, pl.ds(r, devices, stride=16), :] = row[:, r * D:(r + 1) * D]
+        away[:, 16 * s:16 * s + 16, :] = stage[s].astype(BF16).reshape(devices, 16, D)
+    away[:, 32:48, :] = jnp.broadcast_to(tile, (devices, 16, D))
+    pl.semaphore_wait(barrier, devices - 1)
+
+    def send(i, carry):
+        to = lax.rem(me + i, devices)
+        pltpu.make_async_remote_copy(
+            src_ref=away.at[to], dst_ref=arr.at[me], send_sem=send_sem, recv_sem=recv_sem,
+            device_id=place(to), device_id_type=pl.DeviceIdType.MESH,
+        ).start()
+        return carry
+
+    lax.fori_loop(1, devices, send, 0)
+    keep = pltpu.make_async_copy(away.at[me], arr.at[me], in_sem.at[5])
+    keep.start()
+
+    loads[0].wait()
+    loads[1].wait()
+    for s in range(2):
+        res[s] = KEEP * dot3(split(st[s]), split(bs[s]), 1, 0)
+    outs = [pltpu.make_async_copy(res.at[pl.ds(0, 2)], pl_h, out_sem.at[0])]
+    outs[0].start()
+    loads[2].wait()
+    loads[3].wait()
+    for s in range(2):
+        res[2 + s] = KEEP * dot3(split(st[2 + s]), split(bs[2 + s]), 1, 0)
+    outs.append(pltpu.make_async_copy(res.at[pl.ds(2, 2)], pr_h, out_sem.at[1]))
+    outs[1].start()
+    loads[4].wait()
+    for s in range(2):
+        res[4 + s] = dot3(split(dot3(split(bs[s]), split(mo[s]), 0, 0)), split(bs[2 + s]), 1, 0)
+    outs.append(pltpu.make_async_copy(res.at[pl.ds(4, 2)], m2_h, out_sem.at[2]))
+    outs[2].start()
+    keep.wait()
+    most = arr.at[pl.ds(0, devices - 1)]
+    pltpu.make_async_copy(most, most, recv_sem).wait()
+    pltpu.make_async_copy(most, most, send_sem).wait()
+
+    terms = arr[:, 32:48, :].astype(F32)
+    total = jnp.sum(jnp.sum(terms, axis=0), axis=0, keepdims=True)
+    mean = total / (80.0 * N * N)
+    clip_out[...] = jnp.broadcast_to(1.0 / jnp.maximum(1.0, jnp.sqrt(mean)), (8, D))
+    for s in range(2):
+        stage[s] = arr[:, 16 * s:16 * s + 16, :].astype(F32).reshape(16 * devices, D)
+        for q in range(4):
+            for c in range(4):
+                x_s[c, pl.ds(q, D, stride=4), :] = stage[s, pl.ds(4 * q + c, devices, stride=16), :]
+        for c in range(4):
+            g_out[s, :, c * D:(c + 1) * D] = x_s[c].astype(BF16)
+    for c in outs:
+        c.wait()
+
+
+def ahead(code, gradient, left_stat, right_stat, left_basis, right_basis, moment):
+    devices, mp = lax.axis_size(("dp", "mp")), lax.axis_size("mp")
+    vm = pl.BlockSpec(memory_space=pltpu.VMEM)
+    hb = pl.BlockSpec(memory_space=pl.ANY)
     return pl.pallas_call(
-        ahead_kernel,
-        grid=(2,),
-        out_shape=[jax.ShapeDtypeStruct((2, N, N), F32)] * 3,
-        in_specs=[one] * 5,
-        out_specs=[one] * 3,
-        compiler_params=pltpu.CompilerParams(vmem_limit_bytes=56 << 20),
+        functools.partial(ahead_kernel, devices, mp),
+        out_shape=[jax.ShapeDtypeStruct((2, N, N), F32)] * 3
+        + [jax.ShapeDtypeStruct((2, N, N), BF16), jax.ShapeDtypeStruct((8, D), F32)],
+        in_specs=[vm, vm] + [hb] * 5,
+        out_specs=[hb] * 3 + [vm, vm],
+        scratch_shapes=[
+            pltpu.VMEM((2, 16 * devices, D), F32),
+            pltpu.VMEM((devices, 48, D), BF16),
+            pltpu.VMEM((devices, 48, D), BF16),
+            pltpu.VMEM((4, N, D), F32),
+            pltpu.VMEM((4, N, N), F32),
+            pltpu.VMEM((4, N, N), F32),
+            pltpu.VMEM((2, N, N), F32),
+            pltpu.VMEM((6, N, N), F32),
+            pltpu.SemaphoreType.DMA((6,)),
+            pltpu.SemaphoreType.DMA((3,)),
+            pltpu.SemaphoreType.DMA,
+            pltpu.SemaphoreType.DMA,
+        ],
+        compiler_params=pltpu.CompilerParams(
+            vmem_limit_bytes=56 << 20, collective_id=0, has_side_effects=True
+        ),
         cost_estimate=pl.CostEstimate(flops=24 * 2 * N**3, bytes_accessed=16 * N * N * 4, transcendentals=0),
         name="ahead",
-    )(left_stat, right_stat, left_basis, right_basis, moment)
-
-
-def rotate_kernel(live, arr, lb, rb, m2, second, g_out, t_out, u_out, second_out, step_out, clip_out, x_s):
+    )(code, gradient, left_stat, right_stat, left_basis, right_basis, moment)
+
+
+def rotate_kernel(live, clip_in, g_in, lb, rb, m2, second, t_out, u_out, second_out, step_out, x_s):
     s = pl.program_id(0)
     alive = live[s] > 0
-    lanes = lax.broadcasted_iota(jnp.int32, (D, D), 1)
-    terms = jnp.where(lanes < 3, arr[0, :, PIECE:].astype(F32), 0.0)
-    total = jnp.sum(jnp.sum(terms, axis=1, keepdims=True), axis=0, keepdims=True)
-    mean = total / (80.0 * N * N)
-    clip = 1.0 / jnp.maximum(1.0, jnp.sqrt(mean))
-    clip_out[...] = jnp.broadcast_to(clip, (8, D))
-    for q in range(4):
-        for c in range(4):
-            x_s[c, pl.ds(q, D, stride=4), :] = arr[0, :, q * N + c * D:q * N + (c + 1) * D].astype(F32)
-    g = jnp.concatenate([x_s[c] for c in range(4)], axis=1).astype(BF16)
-    g_out[0] = g
+    g = g_in[0]
+    clip = clip_in[0:1, 0:1]
     l, r = split(lb[0]), split(rb[0])
     t = dot2l(l, g, 0, 0)
     t_out[0] = t
@@ -180,34 +265,28 @@
             step_out[0, :, q * N + c * D:q * N + (c + 1) * D] = x_s[c, pl.ds(q, D, stride=4), :]
 
 
-def rotate(live, arrived, left_basis, right_basis, m2, second):
+def rotate(live, clip, g, left_basis, right_basis, m2, second):
     one = pl.BlockSpec((1, N, N), lambda s: (s, 0, 0))
-    width = arrived.shape[-1]
     return pl.pallas_call(
         rotate_kernel,
         grid=(2,),
         out_shape=[
-            jax.ShapeDtypeStruct((2, N, N), BF16),
             jax.ShapeDtypeStruct((2, N, N), F32),
             jax.ShapeDtypeStruct((2, N, N), F32),
             jax.ShapeDtypeStruct((2, N, N), F32),
             jax.ShapeDtypeStruct((2, D, PIECE), F32),
-            jax.ShapeDtypeStruct((8, D), F32),
         ],
         in_specs=[
             pl.BlockSpec(memory_space=pltpu.SMEM),
-            pl.BlockSpec((1, D, width), lambda s: (s, 0, 0)),
-            one, one, one, one,
+            pl.BlockSpec((8, D), lambda s: (0, 0)),
+            one, one, one, one, one,
         ],
-        out_specs=[one] * 4 + [
-            pl.BlockSpec((1, D, PIECE), lambda s: (s, 0, 0)),
-            pl.BlockSpec((8, D), lambda s: (0, 0)),
-        ],
+        out_specs=[one] * 3 + [pl.BlockSpec((1, D, PIECE), lambda s: (s, 0, 0))],
         scratch_shapes=[pltpu.VMEM((4, N, D), F32)],
         compiler_params=pltpu.CompilerParams(vmem_limit_bytes=56 << 20),
         cost_estimate=pl.CostEstimate(flops=30 * 2 * N**3, bytes_accessed=20 * N * N * 4, transcendentals=0),
         name="rotate",
-    )(live, arrived, left_basis, right_basis, m2, second)
+    )(live, clip, g, left_basis, right_basis, m2, second)
 
 
 def refresh_kernel(live, clip_ref, g_ref, t_ref, u_ref, pl_ref, pr_ref, ls_h, rs_h, lb_h, rb_h, m_h,
@@ -298,28 +377,17 @@
     slot_count = left_stat.shape[0]
     flat_piece = gradient.shape[1]
     my_index = lax.axis_index(("dp", "mp"))
-    own_square = jnp.sum(jnp.square(gradient.astype(F32)))
-    first = own_square.astype(BF16)
-    second = (own_square - first.astype(F32)).astype(BF16)
-    third = (own_square - first.astype(F32) - second.astype(F32)).astype(BF16)
-    terms = jnp.stack([first, second, third])
     slot_code = state_slot * devices + owner_device
-    picker = (
-        slot_code[None, :] == jnp.arange(slot_count * devices, dtype=jnp.int32)[:, None]
-    ).astype(BF16)
-    outgoing = jnp.dot(picker, gradient, preferred_element_type=F32).astype(BF16)
-    outgoing = outgoing.reshape(slot_count, devices, flat_piece)
-    tail = jnp.broadcast_to(jnp.pad(terms, (0, 125)), (slot_count, devices, 128))
-    outgoing = jnp.concatenate([outgoing, tail], axis=2)
-    arrived = lax.all_to_all(outgoing, ("dp", "mp"), split_axis=1, concat_axis=1, tiled=True)
-    p_left, p_right, rotated_old = ahead(left_stat, right_stat, left_basis, right_basis, moment)
+    p_left, p_right, rotated_old, g, clip = ahead(
+        slot_code[None, :], gradient, left_stat, right_stat, left_basis, right_basis, moment
+    )
     live = jnp.any(
         (owner_device[None, :] == my_index)
         & (state_slot[None, :] == jnp.arange(slot_count, dtype=jnp.int32)[:, None]),
         axis=1,
     ).astype(jnp.int32)
-    g, t, u, new_second, steps, clip = rotate(
-        live, arrived, left_basis, right_basis, rotated_old, second_moment
+    t, u, new_second, steps = rotate(
+        live, clip, g, left_basis, right_basis, rotated_old, second_moment
     )
     backward = lax.all_to_all(steps, ("dp", "mp"), split_axis=1, concat_axis=1, tiled=True)
     new_left, new_right, new_left_basis, new_right_basis, new_moment = refresh(

time: 115 us -> 115 us (level)
  Pallas kernels: 68.8 us -> 95 us
  starting transfers between devices: 17.5 us -> 7.02 us
  waiting for transfers between devices: 8.44 us -> 0.01 us
  local copies, waits for them, and re-layouts: 10.3 us -> 8.14 us
  other arithmetic: 6.19 us -> 4.11 us
  matrix products: 1.39 us -> 0 us
  between operations: 2.03 us -> 0.69 us
    pallas_call x1, Pallas kernels: 10.4 us -> 36.6 us  [ahead(): pl.pallas_call(functools.partial(ahead_kernel, devices, mp), out_shape=[j...]
    all_to_all x1 -> x0, starting transfers between devices: 11.5 us -> none  [shards(): lax.all_to_all(outgoing, ('dp', 'mp'), split_axis=1, concat_axis=1, tiled...]
    all_to_all x1 -> x0, waiting for transfers between devices: 8.44 us -> none  [shards(): lax.all_to_all(outgoing, ('dp', 'mp'), split_axis=1, concat_axis=1, tiled...]
    concatenate x1 -> x0, other arithmetic: 2.11 us -> none  [shards(): outgoing = jnp.concatenate([outgoing, tail], axis=2)]
    reduce_sum x1 -> x0, other arithmetic: 1.75 us -> none  [shards(): own_square = jnp.sum(jnp.square(gradient.astype(F32)))]
    dot_general x1 -> x0, matrix products: 1.39 us -> none  [shards(): jnp.dot(picker, gradient, preferred_element_type=F32).astype(BF16)]
    broadcast_in_dim x0 -> x1, other arithmetic: none -> 1.19 us  [shards(): slot_code[None, :]]
  transfers between devices with their start and end apart: 2 -> 1, of which waited for: 1 -> 0; matrix products, arithmetic and copies ran while one was open for 1% -> 0% of each run, Pallas kernels for 49% -> 40%
where the time goes in v1:
time: 115 us
  Pallas kernels  95 us (83%)
  local copies, waits for them, and re-layouts  8.14 us (7%)
  starting transfers between devices  7.02 us (6%)
  other arithmetic  4.11 us (4%)
    pallas_call x1, Pallas kernels, refresh(): pl.pallas_call(refresh_kernel, out_shape=[jax.ShapeDtypeStruct((2, N, N),...  45.8 us
    pallas_call x1, Pallas kernels, ahead(): pl.pallas_call(functools.partial(ahead_kernel, devices, mp), out_shape=[j...  36.6 us
    pallas_call x1, Pallas kernels, rotate(): pl.pallas_call(rotate_kernel, grid=(2,), out_shape=[jax.ShapeDtypeStruct(...  12.6 us
    all_to_all x1, starting transfers between devices, shards(): lax.all_to_all(steps, ('dp', 'mp'), split_axis=1, concat_axis=1, tiled=True)  7.02 us
    pallas_call x1, local copies, waits for them, and re-layouts, rotate(): pl.pallas_call(rotate_kernel, grid=(2,), out_shape=[jax.ShapeDtypeStruct(...  4.52 us
    all_to_all x1, local copies, waits for them, and re-layouts, shards(): lax.all_to_all(steps, ('dp', 'mp'), split_axis=1, concat_axis=1, tiled=True)  2.81 us
  transfers between devices with their start and end apart: 1, of which 0 were waited for; matrix products, arithmetic and copies ran while one was open for 0% of the time, Pallas kernels for 40%

profile of v1, /device:TPU:1, one launch (start us, length us, event | category | flops | bytes accessed | tf_op | source)
XLA Modules:
  0.0 115.0 jit_solution(7399403655060877699)
XLA Ops:
  0.6 1.2 %fusion.code = s32[1,80]{1,0:T(1,128)} fusion(s32[80]{0:T(128)} %param.10, s32[80]{0:T(128)} %param.11), kind=kLoop, calls=%fused_computation.8 | loop fusion | flops 160 | bytes 960 | tf_op jit(solution)/shard_map/broadcast_in_dim | solution.py:382
  1.8 0.7 compare_and_fusion
  2.5 0.8 and_reduce_fusion
  3.3 0.5 convert_element_type.3.live
  3.8 36.6 %ahead.1 = (f32[2,512,512]{2,1,0:T(8,128)}, f32[2,512,512]{2,1,0:T(8,128)}, f32[2,512,512]{2,1,0:T(8,128)}, bf16[2,512,512]{2,1,0:T(8,128)(2,1)}, f32[8,128]{1,0:T(8,128)}) custom-call(s32[1,80]{1,0:T(1,128)} %fusion.code, bf16[80,2048]{1,0:T(8,128)(2,1)} %grad.1, f32[2,512,512]{2,1,0:T(8,128)} %ls_h.3, f32[2,512,512]{2,1,0:T(8,128)} %rs_h.3, ...), custom_call_target="tpu_custom_call" | custom-call | flops 6442450944 | bytes 16777216 | tf_op jit(solution)/shard_map/ahead/pallas_call | solution.py:219
  40.4 12.6 %rotate.1 = (f32[2,512,512]{2,1,0:T(8,128)}, f32[2,512,512]{2,1,0:T(8,128)}, f32[2,512,512]{2,1,0:T(8,128)}, f32[2,128,2048]{2,1,0:T(8,128)}) custom-call(s32[2]{0:T(128)} %convert_element_type.3.live, f32[8,128]{1,0:T(8,128)} %get-tuple-element.21.clip_in.clip_ref, bf16[2,512,512]{2,1,0:T(8,128)(2,1)} %get-tuple-element.22.g_in.g_ref, f32[2,512,512]{2,1,0:T(8,128)} %lb_h.3, ...), custom_call_target="tpu_custom_call" | custom-call | flops 8053063680 | bytes 20971520 | tf_op jit(solution)/shard_map/rotate/pallas_call | solution.py:270
  53.0 4.5 %copy.18 = f32[2,128,2048]{2,0,1:T(2,128)} copy(f32[2,128,2048]{2,1,0:T(8,128)} %get-tuple-element.34) | data formatting | bytes 4194304 | tf_op jit(solution)/shard_map/rotate/pallas_call | solution.py:270
  57.5 7.0 %all-to-all-start = ((f32[2,128,2048]{2,0,1:T(2,128)}), f32[2,128,2048]{2,0,1:T(2,128)}, u32[]{:S(2)}, u32[]{:S(2)}) async-start(f32[2,128,2048]{2,0,1:T(2,128)} %copy.18), calls=%async_computation | async-start | bytes 4194304 | tf_op jit(solution)/shard_map/all_to_all | solution.py:392
  64.5 45.8 %refresh.1 = (f32[2,512,512]{2,1,0:T(8,128)}, f32[2,512,512]{2,1,0:T(8,128)}, f32[2,512,512]{2,1,0:T(8,128)}, f32[2,512,512]{2,1,0:T(8,128)}, f32[2,512,512]{2,1,0:T(8,128)}) custom-call(s32[2]{0:T(128)} %convert_element_type.3.live, f32[8,128]{1,0:T(8,128)} %get-tuple-element.21.clip_in.clip_ref, bf16[2,512,512]{2,1,0:T(8,128)(2,1)} %get-tuple-element.22.g_in.g_ref, ...), custom_call_target="tpu_custom_call" | custom-call | flops 26843545600 | bytes 31457280 | tf_op jit(solution)/shard_map/refresh/pallas_call | solution.py:342
  110.4 0.0 all-to-all-done
  110.4 2.8 %copy.19 = f32[2,128,2048]{2,1,0:T(8,128)S(1)} copy(f32[2,128,2048]{2,0,1:T(2,128)} %all-to-all-done) | data formatting | bytes 4194304 | tf_op jit(solution)/shard_map/all_to_all | solution.py:392
  113.2 0.8 gather_fusion
  114.0 0.9 broadcast_select_fusion
  (1 shorter events, 0.0 us)
Async XLA Ops:
  57.5 52.9 %all-to-all-start = ((f32[2,128,2048]{2,0,1:T(2,128)}), f32[2,128,2048]{2,0,1:T(2,128)}, u32[]{:S(2)}, u32[]{:S(2)}) async-start(f32[2,128,2048]{2,0,1:T(2,128)} %copy.18), calls=%async_computation | async-start | bytes 4194304 | tf_op jit(solution)/shard_map/all_to_all | solution.py:392
